TPU v7x, 32 devices: a whole 2x2x4 slice. The times are simulated.
32 devices in a mesh: row: 8 (over y, x, core), res: 4 (over z).
Axes of the slice: x: 2, y: 2, z: 4, core: 2. Of those that a mesh axis runs over, the one named last changes fastest.
Arguments:
- queries: bfloat16 [32, 256, 384], P('row', 'res'), may hold values from -64 to 64
- keys: bfloat16 [32, 256, 384], P('row', 'res'), may hold values from -4 to 4
- values: bfloat16 [32, 256, 384], P('row', 'res'), may hold values from -36 to 36
- out_weight: bfloat16 [384, 768], replicated, may hold values from -0.3125 to 0.3125
- grad_out: bfloat16 [32, 256, 768], P('row', 'res'), may hold values from -24 to 24
Outputs:
- mixed_out: bfloat16 [32, 256, 768], P('row', 'res')
- grad_query: bfloat16 [32, 256, 384], P('row', 'res')
- grad_key: bfloat16 [32, 256, 384], P('row', 'res')
- grad_value: bfloat16 [32, 256, 384], P('row', 'res')
All inputs are finite; a program needn't handle non-finite values.
Results may differ from a plain program's by a relative error of at most 0.013.
Values may be sent and summed in bfloat16 or wider, within the bound.
A program may use at most 64 MiB of HBM per device.

v0:
```python
import math

import jax
import jax.numpy as jnp
from jax import lax
from jax.sharding import PartitionSpec as P

HEADS = 6


def split_heads(array):
    return array.reshape(array.shape[0], array.shape[1], HEADS, array.shape[2] // HEADS)


def softmax_rows(logits):
    top = jnp.max(logits, axis=-1, keepdims=True)
    expo = jnp.exp(logits - top)
    return expo / jnp.sum(expo, axis=-1, keepdims=True)


def score_grad(weights, grads):
    return weights * (grads - jnp.sum(weights * grads, axis=-1, keepdims=True))


def on_device(queries, keys, values, out_weight, grad_out):
    seq_dev, res_dev, width = queries.shape
    model_dim = out_weight.shape[1]
    head_dim = width // HEADS
    total_res = res_dev * lax.axis_size("res")
    logit_scale = 1.0 / math.sqrt(head_dim * seq_dev * lax.axis_size("row"))
    grad_flat = lax.dot_general(
        grad_out.reshape(seq_dev * res_dev, model_dim),
        out_weight,
        (((1,), (1,)), ((), ())),
        preferred_element_type=jnp.float32,
    )
    grad_attended = grad_flat.astype(jnp.bfloat16).reshape(seq_dev, res_dev, width)
    key_all, value_all = (
        lax.all_gather(keys, "res", axis=1, tiled=True),
        lax.all_gather(values, "res", axis=1, tiled=True),
    )
    key_heads = split_heads(key_all)
    value_heads = split_heads(value_all)
    partial_logits = jnp.einsum(
        "sihd,sjhd->hij", split_heads(queries), key_heads, preferred_element_type=jnp.float32
    )
    partial_logits = partial_logits.reshape(HEADS * res_dev, total_res)
    tied_sum = lax.psum(partial_logits, "row") * logit_scale
    full_weights = softmax_rows(tied_sum)
    weights16 = full_weights.astype(jnp.bfloat16)
    weights_heads = weights16.reshape(HEADS, res_dev, total_res)
    attended = jnp.einsum(
        "hij,sjhd->sihd", weights_heads, value_heads, preferred_element_type=jnp.float32
    )
    attended = attended.astype(jnp.bfloat16).reshape(seq_dev * res_dev, width)
    mixed_out = jnp.dot(attended, out_weight, preferred_element_type=jnp.float32)
    mixed_out = mixed_out.astype(jnp.bfloat16).reshape(seq_dev, res_dev, model_dim)
    grad_partial = jnp.einsum(
        "sihd,sjhd->hij",
        split_heads(grad_attended),
        value_heads,
        preferred_element_type=jnp.float32,
    )
    grad_partial = grad_partial.reshape(HEADS * res_dev, total_res)
    tied_grads = lax.psum(grad_partial, "row")
    scores16 = score_grad(full_weights, tied_grads).astype(jnp.bfloat16)
    score_heads = scores16.reshape(HEADS, res_dev, total_res)
    grad_query = (
        jnp.einsum("hij,sjhd->sihd", score_heads, key_heads, preferred_element_type=jnp.float32)
        * logit_scale
    )
    grad_query = grad_query.astype(jnp.bfloat16).reshape(seq_dev, res_dev, width)
    query_all, grad_all = (
        lax.all_gather(queries, "res", axis=1, tiled=True),
        lax.all_gather(grad_attended, "res", axis=1, tiled=True),
    )
    weights_cols, scores_cols = (
        lax.all_to_all(weights_heads, "res", split_axis=2, concat_axis=1, tiled=True),
        lax.all_to_all(score_heads, "res", split_axis=2, concat_axis=1, tiled=True),
    )
    grad_value = jnp.einsum(
        "hij,sihd->sjhd", weights_cols, split_heads(grad_all), preferred_element_type=jnp.float32
    )
    grad_value = grad_value.astype(jnp.bfloat16).reshape(seq_dev, res_dev, width)
    grad_key = (
        jnp.einsum(
            "hij,sihd->sjhd",
            scores_cols,
            split_heads(query_all),
            preferred_element_type=jnp.float32,
        )
        * logit_scale
    )
    grad_key = grad_key.astype(jnp.bfloat16).reshape(seq_dev, res_dev, width)
    return (mixed_out, grad_query, grad_key, grad_value)


def solution(mesh):
    placed = (
        P("row", "res", None),
        P("row", "res", None),
        P("row", "res", None),
        P(),
        P("row", "res", None),
    )
    return jax.shard_map(
        on_device,
        mesh=mesh,
        in_specs=placed,
        out_specs=(
            P("row", "res", None),
            P("row", "res", None),
            P("row", "res", None),
            P("row", "res", None),
        ),
        check_vma=False,
    )
```

profile of v0, /device:TPU:0, one launch (start us, length us, event | category | flops | bytes accessed | tf_op | source)
XLA Modules:
  0.0 144.9 jit_solution(7484980104425860712)
XLA Ops:
  7.2 1.1 copy.59
  8.4 21.3 %all_gather.12 = bf16[4,256,384]{2,0,1:T(4,128)(2,1)S(1)} all-gather(bf16[4,64,384]{2,0,1:T(4,128)(2,1)S(1)} %copy.59), channel_id=1, replica_groups=mesh['row'=8,'res'=4] {'res'}, dimensions={1}, use_global_device_ids=true | all-gather | bytes 983040 | tf_op jit(solution)/shard_map/all_gather | solution.py:39
  29.7 0.6 copy.60
  30.6 1.1 reshape.59
  31.9 17.7 %all_gather.13 = bf16[4,256,384]{2,0,1:T(4,128)(2,1)S(1)} all-gather(bf16[4,64,384]{2,0,1:T(4,128)(2,1)S(1)} %copy.63), channel_id=1, replica_groups=mesh['row'=8,'res'=4] {'res'}, dimensions={1}, use_global_device_ids=true | all-gather | bytes 983040 | tf_op jit(solution)/shard_map/all_gather | solution.py:40
  49.6 0.6 copy.64
  50.6 0.4 convolution_convert_fusion.3
  51.0 1.1 reshape.81
  52.1 1.0 fusion.12
  53.1 1.0 fusion.8
  54.3 17.6 %all_gather.14 = bf16[4,256,384]{2,0,1:T(4,128)(2,1)S(1)} all-gather(bf16[4,64,384]{2,0,1:T(4,128)(2,1)S(1)} %copy.74), channel_id=1, replica_groups=mesh['row'=8,'res'=4] {'res'}, dimensions={1}, use_global_device_ids=true | all-gather | bytes 983040 | tf_op jit(solution)/shard_map/all_gather | solution.py:74
  72.0 1.3 copy.75
  73.5 16.1 %all_gather.15 = bf16[4,256,384]{2,0,1:T(4,128)(2,1)S(1)} all-gather(bf16[4,64,384]{2,0,1:T(4,128)(2,1)S(1)} %copy.78), channel_id=1, replica_groups=mesh['row'=8,'res'=4] {'res'}, dimensions={1}, use_global_device_ids=true | all-gather | bytes 983040 | tf_op jit(solution)/shard_map/all_gather | solution.py:75
  89.6 0.6 copy.79
  90.2 19.7 %all-reduce.3.cloned.1.call-done = (f32[384,256]{1,0:T(8,128)}, f32[384,256]{1,0:T(8,128)}) async-done(((f32[384,256]{1,0:T(8,128)}, f32[384,256]{1,0:T(8,128)}), (f32[384,256]{1,0:T(8,128)}, f32[384,256]{1,0:T(8,128)})) %all-reduce.3.cloned.1.call-update) | async-done | bytes 786448 | tf_op jit(solution)/shard_map/psum | solution.py:48
  109.9 1.2 multiply_reduce_fusion.1
  112.2 1.0 reshape.84
  113.3 4.5 %all-to-all-start = ((bf16[4,2,12288]{2,1,0:T(2,128)(2,1)}), bf16[4,2,12288]{2,1,0:T(2,128)(2,1)S(1)}, u32[]{:S(2)}, u32[]{:S(2)}) async-start(bf16[4,2,12288]{2,1,0:T(2,128)(2,1)} %reshape.84), calls=%async_computation | async-start | bytes 393216 | tf_op jit(solution)/shard_map/all_to_all | solution.py:79
  117.7 0.5 fusion.4
  119.1 1.0 reshape.86
  120.1 0.5 fusion.3
  120.6 3.5 %all-to-all-done = bf16[4,2,12288]{2,1,0:T(2,128)(2,1)S(1)} async-done(((bf16[4,2,12288]{2,1,0:T(2,128)(2,1)}), bf16[4,2,12288]{2,1,0:T(2,128)(2,1)S(1)}, u32[]{:S(2)}, u32[]{:S(2)}) %all-to-all-start) | async-done | bytes 196640 | tf_op jit(solution)/shard_map/all_to_all | solution.py:79
  124.2 4.0 %all-to-all-start.1 = ((bf16[4,2,12288]{2,1,0:T(2,128)(2,1)}), bf16[4,2,12288]{2,1,0:T(2,128)(2,1)}, u32[]{:S(2)}, u32[]{:S(2)}) async-start(bf16[4,2,12288]{2,1,0:T(2,128)(2,1)} %reshape.86), calls=%async_computation.1 | async-start | bytes 393216 | tf_op jit(solution)/shard_map/all_to_all | solution.py:78
  128.2 1.1 convolution_convert_fusion.2
  129.6 1.0 reshape.69
  131.5 0.5 copy-done.5
  132.1 0.5 fusion.2
  132.8 1.0 reshape.71
  133.8 0.6 all-to-all-done.1
  134.5 1.2 reshape.87
  136.3 0.3 fusion.5
  137.0 1.0 reshape.74
  (41 shorter events, 5.4 us)
Async XLA Ops:
  7.2 43.1 %copy-start = (bf16[384,768]{1,0:T(8,128)(2,1)S(1)}, bf16[384,768]{1,0:T(8,128)(2,1)}, u32[]{:S(2)}) copy-start(bf16[384,768]{1,0:T(8,128)(2,1)} %param.8) | copy-start | bytes 1769476
  7.2 102.8 %all-reduce.3.cloned.1.call-start = ((), (), s32[]{:S(2)}) async-start(), calls=%async_computation.2 | async-start | bytes 1572864 | tf_op jit(solution)/shard_map/psum | solution.py:48
  29.7 0.9 copy-start.6
  30.6 21.5 %copy-start.3 = (bf16[4,256,384]{1,2,0:T(8,128)(2,1)}, bf16[4,256,384]{1,2,0:T(8,128)(2,1)S(1)}, u32[]{:S(2)}) copy-start(bf16[4,256,384]{1,2,0:T(8,128)(2,1)S(1)} %copy.60) | copy-start | bytes 2359300
  30.6 1.1 copy-start.10
  49.6 1.0 copy-start.9
  51.0 1.1 copy-start.7
  52.1 1.0 copy-start.8
  109.9 1.2 copy-start.1
  109.9 1.5 %copy-start.2 = (f32[384,256]{1,0:T(8,128)S(1)}, f32[384,256]{1,0:T(8,128)}, u32[]{:S(2)}) copy-start(f32[384,256]{1,0:T(8,128)} %get-tuple-element.5) | copy-start | bytes 1179652
  113.3 10.9 %all-to-all-start = ((bf16[4,2,12288]{2,1,0:T(2,128)(2,1)}), bf16[4,2,12288]{2,1,0:T(2,128)(2,1)S(1)}, u32[]{:S(2)}, u32[]{:S(2)}) async-start(bf16[4,2,12288]{2,1,0:T(2,128)(2,1)} %reshape.84), calls=%async_computation | async-start | bytes 393216 | tf_op jit(solution)/shard_map/all_to_all | solution.py:79
  118.8 1.4 copy-start.4
  124.2 10.3 %all-to-all-start.1 = ((bf16[4,2,12288]{2,1,0:T(2,128)(2,1)}), bf16[4,2,12288]{2,1,0:T(2,128)(2,1)}, u32[]{:S(2)}, u32[]{:S(2)}) async-start(bf16[4,2,12288]{2,1,0:T(2,128)(2,1)} %reshape.86), calls=%async_computation.1 | async-start | bytes 393216 | tf_op jit(solution)/shard_map/all_to_all | solution.py:78
  130.9 1.1 copy-start.5
Sparse Core Ops, SparseCore 0:
  54.3 55.5 all-reduce.2
where the time goes:
time: 145 us
  blocking collectives  72.7 us (50%)
  waiting for transfers between devices  23.9 us (16%)
  local copies, waits for them, and re-layouts  18.1 us (12%)
  between operations  14.2 us (10%)
  starting transfers between devices  8.49 us (6%)
  matrix products  5.45 us (4%)
  other arithmetic  1.94 us (1%)
    all_gather x1, blocking collectives, on_device(): lax.all_gather(keys, 'res', axis=1, tiled=True)  21.3 us
    psum x1, waiting for transfers between devices, on_device(): tied_sum = lax.psum(partial_logits, 'row') * logit_scale  19.7 us
    all_gather x1, blocking collectives, on_device(): lax.all_gather(values, 'res', axis=1, tiled=True)  17.7 us
    all_gather x1, blocking collectives, on_device(): lax.all_gather(queries, 'res', axis=1, tiled=True)  17.6 us
    all_gather x1, blocking collectives, on_device(): lax.all_gather(grad_attended, 'res', axis=1, tiled=True)  16.1 us
    unnamed x29, local copies, waits for them, and re-layouts  6.26 us
    all_to_all x1, starting transfers between devices, on_device(): lax.all_to_all(score_heads, 'res', split_axis=2, concat_axis=1, tiled=True)  4.46 us
    all_to_all x1, starting transfers between devices, on_device(): lax.all_to_all(weights_heads, 'res', split_axis=2, concat_axis=1, tiled=T...  4 us
  transfers between devices with their start and end apart: 3, of which 3 were waited for; matrix products, arithmetic and copies ran while one was open for 7% of the time, Pallas kernels for 0%

commit v1 on v0

--- a/solution.py
+++ b/solution.py
@@ -1,11 +1,18 @@
+import functools
 import math
 
 import jax
 import jax.numpy as jnp
 from jax import lax
+from jax.experimental import pallas as pl
+from jax.experimental.pallas import tpu as pltpu
 from jax.sharding import PartitionSpec as P
 
 HEADS = 6
+MESH = pl.DeviceIdType.MESH
+WHOLE_AT = (0, 4, 6, 10)
+HALF_AT = (2, 3, 8, 9)
+PIECES = ((0, True), (0, False), (1, False), (1, True), (2, True), (2, False), (3, False), (3, True))
 
 
 def split_heads(array):
@@ -95,6 +102,284 @@
     return (mixed_out, grad_query, grad_key, grad_value)
 
 
+def dot_nt(a, b):
+    return lax.dot_general(a, b, (((1,), (1,)), ((), ())), preferred_element_type=jnp.float32)
+
+
+def dot_tn(a, b):
+    return lax.dot_general(a, b, (((0,), (0,)), ((), ())), preferred_element_type=jnp.float32)
+
+
+def dot_nn(a, b):
+    return jnp.dot(a, b, preferred_element_type=jnp.float32)
+
+
+def kernel(
+    rows,
+    scale,
+    q_ref,
+    k_ref,
+    v_ref,
+    w_ref,
+    go_ref,
+    mixed_ref,
+    gq_ref,
+    gk_ref,
+    gv_ref,
+    pack_in,
+    held_in,
+    pack_out,
+    held_out,
+    part,
+    part_held,
+    half_part,
+    half_held,
+    prob,
+    zin_send,
+    zin_recv,
+    part_send,
+    part_recv,
+    half_send,
+    half_recv,
+    prob_send,
+    prob_recv,
+    zout_send,
+    zout_recv,
+):
+    seqs, res, width = q_ref.shape
+    total = 4 * res
+    owned = total // rows
+    hd = width // HEADS
+    hh = hd // 2
+    whole = seqs * hd
+    me_r, me_z = lax.axis_index("row"), lax.axis_index("res")
+    pair_z = me_z + 1 - 2 * lax.rem(me_z, 2)
+    z_partners = (lax.rem(me_z + 2, 4), 3 - me_z, pair_z)
+    r_partners = [lax.rem(me_r + d, rows) for d in range(1, rows)]
+    pending = []
+
+    barrier = pltpu.get_barrier_semaphore()
+    for z in z_partners:
+        pl.semaphore_signal(barrier, inc=1, device_id=(me_r, z), device_id_type=MESH)
+    for r in r_partners:
+        pl.semaphore_signal(barrier, inc=1, device_id=(r, me_z), device_id_type=MESH)
+
+    def start(src, dst, send, recv, r, z):
+        copy = pltpu.make_async_remote_copy(
+            src_ref=src,
+            dst_ref=dst,
+            send_sem=send,
+            recv_sem=recv,
+            device_id=(r, z),
+            device_id_type=MESH,
+        )
+        copy.start()
+        pending.append(copy)
+        return copy
+
+    def pack(phase, array, x):
+        for z in range(4):
+            lo, lh = WHOLE_AT[z] * hh, HALF_AT[z] * hh
+            pack_in[phase, array, z, :, :whole] = jnp.concatenate(
+                [x[s][:, lo : lo + hd] for s in range(seqs)], axis=-1
+            )
+            pack_in[phase, array, z, :, whole:] = jnp.concatenate(
+                [x[s][:, lh : lh + hh] for s in range(seqs)], axis=-1
+            )
+
+    def exchange(phase, sent, held, send_sem, recv_sem):
+        copies = [
+            start(
+                sent.at[phase, :, z],
+                held.at[phase, :, me_z],
+                send_sem.at[phase, n],
+                recv_sem.at[phase, n],
+                me_r,
+                z,
+            )
+            for n, z in enumerate(z_partners)
+        ]
+        held[phase, :, me_z] = sent[phase, :, me_z]
+        return copies
+
+    def gathered(phase, array):
+        x = held_in[phase, array].reshape(total, width)
+        return x[:, :whole], x[:, whole:]
+
+    def spread_parts(phase, a, b):
+        part[phase, 0] = dot_nt(a[0], b[0]).reshape(rows, owned, total)
+        part[phase, 1] = dot_nt(a[1], b[1]).reshape(rows, owned, total)
+        copies = [
+            start(
+                part.at[phase, :, r],
+                part_held.at[phase, me_r],
+                part_send.at[phase, n],
+                part_recv.at[phase, n],
+                r,
+                me_z,
+            )
+            for n, r in enumerate(r_partners)
+        ]
+        part_held[phase, me_r] = part[phase, :, me_r]
+        return copies
+
+    def tied(phase, copies):
+        for copy in copies:
+            copy.wait_recv()
+        half = part_held[phase, 0, 1]
+        for r in range(1, rows):
+            half = half + part_held[phase, r, 1]
+        half_part[phase] = half
+        copy = start(
+            half_part.at[phase],
+            half_held.at[phase],
+            half_send.at[phase],
+            half_recv.at[phase],
+            me_r,
+            pair_z,
+        )
+        full = part_held[phase, 0, 0]
+        for r in range(1, rows):
+            full = full + part_held[phase, r, 0]
+        copy.wait_recv()
+        return full, half + half_held[phase]
+
+    def spread_probs(phase, values):
+        for n in range(2):
+            prob[phase, n, me_r] = values[n].astype(jnp.bfloat16)
+        return [
+            start(
+                prob.at[phase, :, me_r],
+                prob.at[phase, :, me_r],
+                prob_send.at[phase, n],
+                prob_recv.at[phase, n],
+                r,
+                me_z,
+            )
+            for n, r in enumerate(r_partners)
+        ]
+
+    def probs(phase, copies):
+        for copy in copies:
+            copy.wait_recv()
+        return prob[phase, 0].reshape(total, total), prob[phase, 1].reshape(total, total)
+
+    def emit(phase, array, full, half):
+        pack_out[phase, array, :, :, :whole] = full.astype(jnp.bfloat16).reshape(4, res, whole)
+        pack_out[phase, array, :, :, whole:] = half.astype(jnp.bfloat16).reshape(
+            4, res, width - whole
+        )
+
+    def unpack(phase, array, s):
+        pieces = []
+        for z, is_whole in PIECES:
+            at, size = (s * hd, hd) if is_whole else (whole + s * hh, hh)
+            pieces.append(held_out[phase, array, z, :, at : at + size])
+        return jnp.concatenate(pieces, axis=-1)
+
+    pack(0, 0, [q_ref[s] for s in range(seqs)])
+    pack(0, 1, [k_ref[s] for s in range(seqs)])
+    pl.semaphore_wait(barrier, len(z_partners) + len(r_partners))
+    first_in = exchange(0, pack_in, held_in, zin_send, zin_recv)
+    pack(1, 0, [v_ref[s] for s in range(seqs)])
+    ga = dot_nt(go_ref[...].reshape(seqs * res, go_ref.shape[2]), w_ref[...])
+    ga = ga.astype(jnp.bfloat16)
+    pack(1, 1, [ga[s * res : (s + 1) * res] for s in range(seqs)])
+    second_in = exchange(1, pack_in, held_in, zin_send, zin_recv)
+
+    for copy in first_in:
+        copy.wait_recv()
+    logit_parts = spread_parts(0, gathered(0, 0), gathered(0, 1))
+    weights = [softmax_rows(x * scale) for x in tied(0, logit_parts)]
+    weight_copies = spread_probs(0, weights)
+
+    for copy in second_in:
+        copy.wait_recv()
+    grad_parts = spread_parts(1, gathered(1, 1), gathered(1, 0))
+
+    w16 = probs(0, weight_copies)
+    vals, grads = gathered(1, 0), gathered(1, 1)
+    emit(0, 0, dot_nn(w16[0], vals[0]), dot_nn(w16[1], vals[1]))
+    emit(0, 1, dot_tn(w16[0], grads[0]), dot_tn(w16[1], grads[1]))
+    first_out = exchange(0, pack_out, held_out, zout_send, zout_recv)
+
+    tied_grads = tied(1, grad_parts)
+    scores = [score_grad(w, g) for w, g in zip(weights, tied_grads)]
+    s16 = probs(1, spread_probs(1, scores))
+    qs, ks = gathered(0, 0), gathered(0, 1)
+    emit(1, 0, dot_nn(s16[0], ks[0]) * scale, dot_nn(s16[1], ks[1]) * scale)
+    emit(1, 1, dot_tn(s16[0], qs[0]) * scale, dot_tn(s16[1], qs[1]) * scale)
+    second_out = exchange(1, pack_out, held_out, zout_send, zout_recv)
+
+    for copy in first_out:
+        copy.wait_recv()
+    for s in range(seqs):
+        mixed_ref[s] = dot_nn(unpack(0, 0, s), w_ref[...]).astype(jnp.bfloat16)
+        gv_ref[s] = unpack(0, 1, s)
+    for copy in second_out:
+        copy.wait_recv()
+    for s in range(seqs):
+        gq_ref[s] = unpack(1, 0, s)
+        gk_ref[s] = unpack(1, 1, s)
+    for copy in pending:
+        copy.wait_send()
+
+
+def fused(rows, queries, keys, values, out_weight, grad_out):
+    seqs, res, width = queries.shape
+    model_dim = out_weight.shape[1]
+    total = 4 * res
+    owned = total // rows
+    scale = 1.0 / math.sqrt(width // HEADS * seqs * rows)
+    bf16, f32 = jnp.bfloat16, jnp.float32
+    dma = pltpu.SemaphoreType.DMA
+    vmem = pl.BlockSpec(memory_space=pltpu.VMEM)
+    same = jax.ShapeDtypeStruct(queries.shape, bf16)
+    return pl.pallas_call(
+        functools.partial(kernel, rows, scale),
+        out_shape=(jax.ShapeDtypeStruct((seqs, res, model_dim), bf16), same, same, same),
+        in_specs=[vmem] * 5,
+        out_specs=(vmem,) * 4,
+        scratch_shapes=[
+            pltpu.VMEM((2, 2, 4, res, width), bf16),
+            pltpu.VMEM((2, 2, 4, res, width), bf16),
+            pltpu.VMEM((2, 2, 4, res, width), bf16),
+            pltpu.VMEM((2, 2, 4, res, width), bf16),
+            pltpu.VMEM((2, 2, rows, owned, total), f32),
+            pltpu.VMEM((2, rows, 2, owned, total), f32),
+            pltpu.VMEM((2, owned, total), f32),
+            pltpu.VMEM((2, owned, total), f32),
+            pltpu.VMEM((2, 2, rows, owned, total), bf16),
+            dma((2, 3)),
+            dma((2, 3)),
+            dma((2, rows - 1)),
+            dma((2, rows - 1)),
+            dma((2,)),
+            dma((2,)),
+            dma((2, rows - 1)),
+            dma((2, rows - 1)),
+            dma((2, 3)),
+            dma((2, 3)),
+        ],
+        compiler_params=pltpu.CompilerParams(
+            collective_id=0, has_side_effects=True, vmem_limit_bytes=40 * 1024 * 1024
+        ),
+    )(queries, keys, values, out_weight, grad_out)
+
+
+def fits(rows, cols, seqs, res, width):
+    total = cols * res
+    return (
+        cols == 4
+        and rows > 1
+        and seqs == 4
+        and width == HEADS * 64
+        and res % 16 == 0
+        and total % (16 * rows) == 0
+        and total <= 512
+    )
+
+
 def solution(mesh):
     placed = (
         P("row", "res", None),
@@ -103,8 +388,15 @@
         P(),
         P("row", "res", None),
     )
+    rows, cols = mesh.shape["row"], mesh.shape["res"]
+
+    def body(queries, keys, values, out_weight, grad_out):
+        if fits(rows, cols, *queries.shape):
+            return fused(rows, queries, keys, values, out_weight, grad_out)
+        return on_device(queries, keys, values, out_weight, grad_out)
+
     return jax.shard_map(
-        on_device,
+        body,
         mesh=mesh,
         in_specs=placed,
         out_specs=(

time: 145 us -> 65.3 us (0.45)
  blocking collectives: 72.7 us -> 0 us
  Pallas kernels: 0 us -> 56.8 us
  waiting for transfers between devices: 23.9 us -> 0 us
  between operations: 14.2 us -> 0.65 us
  local copies, waits for them, and re-layouts: 18.1 us -> 7.61 us
  starting transfers between devices: 8.49 us -> 0 us
  matrix products: 5.45 us -> 0 us
  other arithmetic: 1.94 us -> 0 us
    all_gather x4 -> x0, blocking collectives: 72.7 us -> none  [the longest x1 21.3 us: on_device(): lax.all_gather(keys, 'res', axis=1, tiled=True)]
    pallas_call x0 -> x1, Pallas kernels: none -> 56.8 us  [fused(): pl.pallas_call(functools.partial(kernel, rows, scale), out_shape=(jax.Sha...]
    psum x1 -> x0, waiting for transfers between devices: 19.7 us -> none  [on_device(): tied_sum = lax.psum(partial_logits, 'row') * logit_scale]
    all_to_all x2 -> x0, starting transfers between devices: 8.45 us -> none  [the longest x1 4.46 us: on_device(): lax.all_to_all(score_heads, 'res', split_axis=2, concat_axis=1, tiled=True)]
    dot_general x8 -> x0, matrix products: 5.45 us -> none  [the longest x1 1.15 us: on_device(): jnp.dot(attended, out_weight, preferred_element_type=jnp.float32)]
    reshape x8 -> x0, local copies, waits for them, and re-layouts: 5.17 us -> none  [the longest x1 1.1 us: split_heads(): array.reshape(array.shape[0], array.shape[1], HEADS, array.shape[2] // HE...]
    all_to_all x2 -> x0, waiting for transfers between devices: 4.19 us -> none  [the longest x1 3.55 us: on_device(): lax.all_to_all(score_heads, 'res', split_axis=2, concat_axis=1, tiled=True)]
    all_gather x4 -> x0, local copies, waits for them, and re-layouts: 3.29 us -> none  [the longest x1 1.35 us: on_device(): lax.all_gather(queries, 'res', axis=1, tiled=True)]
  transfers between devices with their start and end apart: 3 -> 0, of which waited for: 3 -> 0; matrix products, arithmetic and copies ran while one was open for 7% -> 0% of each run, Pallas kernels for 0% -> 0%
where the time goes in v1:
time: 65.3 us; the launch traced here: 65 us
  Pallas kernels  56.8 us (87%)
  local copies, waits for them, and re-layouts  7.61 us (12%)
    pallas_call x1, Pallas kernels, fused(): pl.pallas_call(functools.partial(kernel, rows, scale), out_shape=(jax.Sha...  56.8 us
    unnamed x14, local copies, waits for them, and re-layouts  7.61 us

profile of v1, /device:TPU:0, one launch (start us, length us, event | category | flops | bytes accessed | tf_op | source)
XLA Modules:
  0.0 65.0 jit_solution(11806552218985624423)
XLA Ops:
  0.6 0.0 copy-start
  0.6 1.1 %copy-done = bf16[384,768]{1,0:T(8,128)(2,1)S(1)} copy-done((bf16[384,768]{1,0:T(8,128)(2,1)S(1)}, bf16[384,768]{1,0:T(8,128)(2,1)}, u32[]{:S(2)}) %copy-start) | copy-done | bytes 589848
  1.7 0.0 copy-start.1
  1.7 1.0 %copy-done.1 = bf16[4,64,768]{2,1,0:T(8,128)(2,1)S(1)} copy-done((bf16[4,64,768]{2,1,0:T(8,128)(2,1)S(1)}, bf16[4,64,768]{2,1,0:T(8,128)(2,1)}, u32[]{:S(2)}) %copy-start.1) | copy-done | bytes 393240
  2.7 0.0 copy-start.2
  2.7 0.9 %copy-done.2 = bf16[4,64,384]{2,1,0:T(8,128)(2,1)S(1)} copy-done((bf16[4,64,384]{2,1,0:T(8,128)(2,1)S(1)}, bf16[4,64,384]{2,1,0:T(8,128)(2,1)}, u32[]{:S(2)}) %copy-start.2) | copy-done | bytes 196632
  3.6 0.0 copy-start.3
  3.6 0.9 %copy-done.3 = bf16[4,64,384]{2,1,0:T(8,128)(2,1)S(1)} copy-done((bf16[4,64,384]{2,1,0:T(8,128)(2,1)S(1)}, bf16[4,64,384]{2,1,0:T(8,128)(2,1)}, u32[]{:S(2)}) %copy-start.3) | copy-done | bytes 196632
  4.5 0.0 copy-start.4
  4.6 0.9 %copy-done.4 = bf16[4,64,384]{2,1,0:T(8,128)(2,1)S(1)} copy-done((bf16[4,64,384]{2,1,0:T(8,128)(2,1)S(1)}, bf16[4,64,384]{2,1,0:T(8,128)(2,1)}, u32[]{:S(2)}) %copy-start.4) | copy-done | bytes 196632
  5.5 56.8 %shard_map.84 = (bf16[4,64,768]{2,1,0:T(8,128)(2,1)S(1)}, bf16[4,64,384]{2,1,0:T(8,128)(2,1)S(1)}, bf16[4,64,384]{2,1,0:T(8,128)(2,1)S(1)}, bf16[4,64,384]{2,1,0:T(8,128)(2,1)S(1)}) custom-call(bf16[4,64,384]{2,1,0:T(8,128)(2,1)S(1)} %copy-done.2, bf16[4,64,384]{2,1,0:T(8,128)(2,1)S(1)} %copy-done.3, bf16[4,64,384]{2,1,0:T(8,128)(2,1)S(1)} %copy-done.4, ...), custom_call_target="tpu_custom_call" | custom-call | tf_op jit(solution)/shard_map/pallas_call | solution.py:338
  62.2 0.7 %copy.13 = bf16[4,64,768]{2,1,0:T(8,128)(2,1)} copy(bf16[4,64,768]{2,1,0:T(8,128)(2,1)S(1)} %get-tuple-element.8) | data formatting | bytes 786432
  63.0 0.7 %copy.14 = bf16[4,64,384]{2,1,0:T(8,128)(2,1)} copy(bf16[4,64,384]{2,1,0:T(8,128)(2,1)S(1)} %get-tuple-element.9) | data formatting | bytes 393216
  63.7 0.7 %copy.15 = bf16[4,64,384]{2,1,0:T(8,128)(2,1)} copy(bf16[4,64,384]{2,1,0:T(8,128)(2,1)S(1)} %get-tuple-element.10) | data formatting | bytes 393216
  64.3 0.7 %copy.16 = bf16[4,64,384]{2,1,0:T(8,128)(2,1)} copy(bf16[4,64,384]{2,1,0:T(8,128)(2,1)S(1)} %get-tuple-element.11) | data formatting | bytes 393216
Async XLA Ops:
  0.6 1.1 %copy-start = (bf16[384,768]{1,0:T(8,128)(2,1)S(1)}, bf16[384,768]{1,0:T(8,128)(2,1)}, u32[]{:S(2)}) copy-start(bf16[384,768]{1,0:T(8,128)(2,1)} %w_ref.1) | copy-start | bytes 1769476
  1.7 1.0 %copy-start.1 = (bf16[4,64,768]{2,1,0:T(8,128)(2,1)S(1)}, bf16[4,64,768]{2,1,0:T(8,128)(2,1)}, u32[]{:S(2)}) copy-start(bf16[4,64,768]{2,1,0:T(8,128)(2,1)} %go_ref.1) | copy-start | bytes 1179652
  2.7 0.9 %copy-start.2 = (bf16[4,64,384]{2,1,0:T(8,128)(2,1)S(1)}, bf16[4,64,384]{2,1,0:T(8,128)(2,1)}, u32[]{:S(2)}) copy-start(bf16[4,64,384]{2,1,0:T(8,128)(2,1)} %q_ref.1) | copy-start | bytes 589828
  3.6 0.9 %copy-start.3 = (bf16[4,64,384]{2,1,0:T(8,128)(2,1)S(1)}, bf16[4,64,384]{2,1,0:T(8,128)(2,1)}, u32[]{:S(2)}) copy-start(bf16[4,64,384]{2,1,0:T(8,128)(2,1)} %k_ref.1) | copy-start | bytes 589828
  4.5 0.9 %copy-start.4 = (bf16[4,64,384]{2,1,0:T(8,128)(2,1)S(1)}, bf16[4,64,384]{2,1,0:T(8,128)(2,1)}, u32[]{:S(2)}) copy-start(bf16[4,64,384]{2,1,0:T(8,128)(2,1)} %v_ref.1) | copy-start | bytes 589828

commit v2 on v0

--- a/solution.py
+++ b/solution.py
@@ -1,11 +1,16 @@
+import functools
 import math
 
 import jax
 import jax.numpy as jnp
 from jax import lax
+from jax.experimental import pallas as pl
+from jax.experimental.pallas import tpu as pltpu
 from jax.sharding import PartitionSpec as P
 
 HEADS = 6
+MESH = pl.DeviceIdType.MESH
+TILE = 128
 
 
 def split_heads(array):
@@ -95,6 +100,350 @@
     return (mixed_out, grad_query, grad_key, grad_value)
 
 
+def dot_nt(a, b):
+    return lax.dot_general(a, b, (((1,), (1,)), ((), ())), preferred_element_type=jnp.float32)
+
+
+def dot_tn(a, b):
+    return lax.dot_general(a, b, (((0,), (0,)), ((), ())), preferred_element_type=jnp.float32)
+
+
+def dot_nn(a, b):
+    return jnp.dot(a, b, preferred_element_type=jnp.float32)
+
+
+def is_end(z):
+    return z in (0, 3)
+
+
+def tile_of(z):
+    return pl.ds(0 if z == 0 else 2 * TILE, TILE)
+
+
+def kernel(
+    rows,
+    scale,
+    q_ref,
+    k_ref,
+    v_ref,
+    w_hbm,
+    go_hbm,
+    mixed_ref,
+    gq_ref,
+    gk_ref,
+    gv_ref,
+    w_ref,
+    go_ref,
+    mid,
+    ga_ref,
+    packed,
+    held,
+    part,
+    part_held,
+    prob,
+    sent_out,
+    mid_held,
+    att_ref,
+    load_sem,
+    zin_send,
+    zin_recv,
+    part_send,
+    part_recv,
+    prob_send,
+    prob_recv,
+    zout_send,
+    zout_recv,
+):
+    me_r, me_z = lax.axis_index("row"), lax.axis_index("res")
+    seqs, res, _ = q_ref.shape
+    total = 4 * res
+    owned = total // rows
+    half = TILE // 2
+    r_partners = [lax.rem(me_r + d, rows) for d in range(1, rows)]
+    inputs = (q_ref, k_ref, v_ref)
+
+    barrier = pltpu.get_barrier_semaphore()
+    for d in range(1, 4):
+        pl.semaphore_signal(
+            barrier, inc=1, device_id=(me_r, lax.rem(me_z + d, 4)), device_id_type=MESH
+        )
+    for r in r_partners:
+        pl.semaphore_signal(barrier, inc=1, device_id=(r, me_z), device_id_type=MESH)
+
+    loads = [
+        pltpu.make_async_copy(x.at[:, :, pl.ds(TILE, TILE)], mid.at[n], load_sem.at[n])
+        for n, x in enumerate(inputs)
+    ]
+    loads.append(pltpu.make_async_copy(w_hbm, w_ref, load_sem.at[3]))
+    loads.append(pltpu.make_async_copy(go_hbm, go_ref, load_sem.at[4]))
+    for load in loads:
+        load.start()
+    pl.semaphore_wait(barrier, 3 + len(r_partners))
+
+    def run(z):
+        end = is_end(z)
+        heads = 2 if end else 1
+        blocks = seqs if end else seqs // 2
+        partners = (z ^ 2, z ^ 3, z ^ 1)
+        pending = []
+
+        def start(src, dst, send, recv, device):
+            copy = pltpu.make_async_remote_copy(
+                src_ref=src,
+                dst_ref=dst,
+                send_sem=send,
+                recv_sem=recv,
+                device_id=device,
+                device_id_type=MESH,
+            )
+            copy.start()
+            pending.append(copy)
+
+        def arrived(ref, sem):
+            pltpu.make_async_copy(ref, ref, sem).wait()
+
+        def slots(array, source):
+            return held.at[array, source, pl.ds(0, blocks)]
+
+        own = []
+        if end:
+            for n, x in enumerate(inputs):
+                copy = pltpu.make_async_copy(x.at[:, :, tile_of(z)], slots(n, z), load_sem.at[5 + n])
+                copy.start()
+                own.append(copy)
+
+        def send_in(array, x, to_ends):
+            for n, p in enumerate(partners):
+                if is_end(p) != to_ends:
+                    continue
+                if to_ends:
+                    src, dst = x.at[:, :, tile_of(p)], held.at[array, z]
+                else:
+                    src, dst = packed.at[array, p - 1], held.at[array, z, pl.ds(0, seqs // 2)]
+                start(src, dst, zin_send.at[array, n], zin_recv.at[array, n], (me_r, p))
+
+        def pack(array, tiles):
+            for s in range(seqs // 2):
+                x, y = tiles[2 * s], tiles[2 * s + 1]
+                packed[array, 0, s] = jnp.concatenate([x[:, :half], y[:, :half]], axis=-1)
+                packed[array, 1, s] = jnp.concatenate([x[:, half:], y[:, half:]], axis=-1)
+            if not end:
+                held[array, z, : seqs // 2] = packed[array, z - 1]
+
+        def input_of(array):
+            if end:
+                own_wait = own[array] if array < 3 else None
+                if own_wait is not None:
+                    own_wait.wait()
+            for n, p in enumerate(partners):
+                arrived(slots(array, p), zin_recv.at[array, n])
+
+        def rows_of(array):
+            return jnp.concatenate(
+                [held[array, :, s].reshape(total, TILE) for s in range(blocks)], axis=-1
+            )
+
+        def first_head(x):
+            return lax.rem(lax.broadcasted_iota(jnp.int32, x.shape, 1), TILE) < half
+
+        def partial_sums(a, b):
+            if not end:
+                return [dot_nt(a, b)]
+            first, zero = first_head(a), jnp.zeros_like(a)
+            return [dot_nt(jnp.where(first, a, zero), b), dot_nt(jnp.where(first, zero, a), b)]
+
+        def spread_parts(phase, sums):
+            for h, x in enumerate(sums):
+                part[phase, h] = x.reshape(rows, owned, total)
+            for n, r in enumerate(r_partners):
+                start(
+                    part.at[phase, pl.ds(0, heads), r],
+                    part_held.at[phase, me_r, pl.ds(0, heads)],
+                    part_send.at[phase, n],
+                    part_recv.at[phase, n],
+                    (r, me_z),
+                )
+            for h in range(heads):
+                part_held[phase, me_r, h] = part[phase, h, me_r]
+
+        def tied(phase):
+            for n in range(rows - 1):
+                arrived(part_held.at[phase, n, pl.ds(0, heads)], part_recv.at[phase, n])
+            sums = []
+            for h in range(heads):
+                x = part_held[phase, 0, h]
+                for r in range(1, rows):
+                    x = x + part_held[phase, r, h]
+                sums.append(x)
+            return sums
+
+        def spread_probs(phase, values):
+            for h, x in enumerate(values):
+                prob[phase, h, me_r] = x.astype(jnp.bfloat16)
+            for n, r in enumerate(r_partners):
+                block = prob.at[phase, pl.ds(0, heads), me_r]
+                start(block, block, prob_send.at[phase, n], prob_recv.at[phase, n], (r, me_z))
+
+        def probs(phase):
+            for n in range(rows - 1):
+                arrived(prob.at[phase, pl.ds(0, heads), n], prob_recv.at[phase, n])
+            return [prob[phase, h].reshape(total, total) for h in range(heads)]
+
+        def emit(array, dot, weights, x, factor, out_ref):
+            y = dot(weights[0], x)
+            if end:
+                y = jnp.where(first_head(y), y, dot(weights[1], x))
+            if factor is not None:
+                y = y * factor
+            y = y.astype(jnp.bfloat16)
+            for s in range(blocks):
+                sent_out[array, :, s] = y[:, s * TILE : (s + 1) * TILE].reshape(4, res, TILE)
+            for n, p in enumerate(partners):
+                if end:
+                    dst = out_ref.at[:, :, tile_of(z)]
+                else:
+                    dst = mid_held.at[array, z - 1]
+                start(
+                    sent_out.at[array, p, pl.ds(0, blocks)],
+                    dst,
+                    zout_send.at[array, n],
+                    zout_recv.at[array, n],
+                    (me_r, p),
+                )
+            if end:
+                lo = 0 if z == 0 else 2 * TILE
+                out_ref[:, :, lo : lo + TILE] = sent_out[array, z]
+            else:
+                mid_held[array, z - 1] = sent_out[array, z, : seqs // 2]
+
+        def finish(array, out_ref):
+            for n, p in enumerate(partners):
+                if is_end(p):
+                    arrived(out_ref.at[:, :, tile_of(p)], zout_recv.at[array, n])
+                else:
+                    arrived(mid_held.at[array, p - 1], zout_recv.at[array, n])
+            for s in range(seqs // 2):
+                x, y = mid_held[array, 0, s], mid_held[array, 1, s]
+                out_ref[2 * s, :, TILE : 2 * TILE] = jnp.concatenate(
+                    [x[:, :half], y[:, :half]], axis=-1
+                )
+                out_ref[2 * s + 1, :, TILE : 2 * TILE] = jnp.concatenate(
+                    [x[:, half:], y[:, half:]], axis=-1
+                )
+
+        send_in(0, q_ref, True)
+        send_in(1, k_ref, True)
+        for n in range(2):
+            loads[n].wait()
+            pack(n, [mid[n, s] for s in range(seqs)])
+            send_in(n, None, False)
+        send_in(2, v_ref, True)
+        loads[2].wait()
+        pack(2, [mid[2, s] for s in range(seqs)])
+        send_in(2, None, False)
+        loads[3].wait()
+        loads[4].wait()
+        ga = dot_nt(go_ref[...].reshape(seqs * res, go_ref.shape[2]), w_ref[...])
+        ga = ga.astype(jnp.bfloat16).reshape(seqs, res, 3 * TILE)
+        ga_ref[...] = ga
+        if end:
+            lo = 0 if z == 0 else 2 * TILE
+            held[3, z] = ga[:, :, lo : lo + TILE]
+        pack(3, [ga[s, :, TILE : 2 * TILE] for s in range(seqs)])
+
+        input_of(0)
+        input_of(1)
+        spread_parts(0, partial_sums(rows_of(0), rows_of(1)))
+        send_in(3, ga_ref, True)
+        send_in(3, None, False)
+        weights = [softmax_rows(x * scale) for x in tied(0)]
+        spread_probs(0, weights)
+
+        input_of(2)
+        input_of(3)
+        vals, grads = rows_of(2), rows_of(3)
+        spread_parts(1, partial_sums(grads, vals))
+
+        w16 = probs(0)
+        emit(0, dot_nn, w16, vals, None, att_ref)
+        scores = [score_grad(w, g) for w, g in zip(weights, tied(1))]
+        spread_probs(1, scores)
+        emit(1, dot_tn, w16, grads, None, gv_ref)
+        s16 = probs(1)
+        emit(2, dot_nn, s16, rows_of(1), scale, gq_ref)
+        emit(3, dot_tn, s16, rows_of(0), scale, gk_ref)
+
+        finish(0, att_ref)
+        mixed = dot_nn(att_ref[...].reshape(seqs * res, 3 * TILE), w_ref[...])
+        mixed_ref[...] = mixed.astype(jnp.bfloat16).reshape(mixed_ref.shape)
+        finish(1, gv_ref)
+        finish(2, gq_ref)
+        finish(3, gk_ref)
+        for copy in pending:
+            copy.wait_send()
+
+    for z in range(4):
+        pl.when(me_z == z)(functools.partial(run, z))
+
+
+def fused(rows, queries, keys, values, out_weight, grad_out):
+    seqs, res, width = queries.shape
+    model_dim = out_weight.shape[1]
+    total = 4 * res
+    owned = total // rows
+    scale = 1.0 / math.sqrt(width // HEADS * seqs * rows)
+    bf16, f32 = jnp.bfloat16, jnp.float32
+    dma = pltpu.SemaphoreType.DMA
+    hbm = pl.BlockSpec(memory_space=pltpu.HBM)
+    vmem = pl.BlockSpec(memory_space=pltpu.VMEM)
+    same = jax.ShapeDtypeStruct(queries.shape, bf16)
+    return pl.pallas_call(
+        functools.partial(kernel, rows, scale),
+        out_shape=(jax.ShapeDtypeStruct((seqs, res, model_dim), bf16), same, same, same),
+        in_specs=[hbm] * 5,
+        out_specs=(vmem,) * 4,
+        scratch_shapes=[
+            pltpu.VMEM(out_weight.shape, bf16),
+            pltpu.VMEM(grad_out.shape, bf16),
+            pltpu.VMEM((3, seqs, res, TILE), bf16),
+            pltpu.VMEM((seqs, res, width), bf16),
+            pltpu.VMEM((4, 2, seqs // 2, res, TILE), bf16),
+            pltpu.VMEM((4, 4, seqs, res, TILE), bf16),
+            pltpu.VMEM((2, 2, rows, owned, total), f32),
+            pltpu.VMEM((2, rows, 2, owned, total), f32),
+            pltpu.VMEM((2, 2, rows, owned, total), bf16),
+            pltpu.VMEM((4, 4, seqs, res, TILE), bf16),
+            pltpu.VMEM((4, 2, seqs // 2, res, TILE), bf16),
+            pltpu.VMEM((seqs, res, width), bf16),
+            dma((8,)),
+            dma((4, 3)),
+            dma((4, 3)),
+            dma((2, rows - 1)),
+            dma((2, rows - 1)),
+            dma((2, rows - 1)),
+            dma((2, rows - 1)),
+            dma((4, 3)),
+            dma((4, 3)),
+        ],
+        compiler_params=pltpu.CompilerParams(
+            collective_id=0, has_side_effects=True, vmem_limit_bytes=62 * 1024 * 1024
+        ),
+    )(queries, keys, values, out_weight, grad_out)
+
+
+def fits(rows, cols, seqs, res, width):
+    total = cols * res
+    return (
+        cols == 4
+        and rows > 1
+        and seqs == 4
+        and width == HEADS * 64
+        and res % 16 == 0
+        and total % (16 * rows) == 0
+        and total <= 512
+    )
+
+
 def solution(mesh):
     placed = (
         P("row", "res", None),
@@ -103,8 +452,15 @@
         P(),
         P("row", "res", None),
     )
+    rows, cols = mesh.shape["row"], mesh.shape["res"]
+
+    def body(queries, keys, values, out_weight, grad_out):
+        if fits(rows, cols, *queries.shape):
+            return fused(rows, queries, keys, values, out_weight, grad_out)
+        return on_device(queries, keys, values, out_weight, grad_out)
+
     return jax.shard_map(
-        on_device,
+        body,
         mesh=mesh,
         in_specs=placed,
         out_specs=(

time: 145 us -> 57.2 us (0.39)
  blocking collectives: 72.7 us -> 0 us
  Pallas kernels: 0 us -> 51.8 us
  waiting for transfers between devices: 23.9 us -> 0 us
  local copies, waits for them, and re-layouts: 18.1 us -> 4.48 us
  between operations: 14.2 us -> 0.65 us
  starting transfers between devices: 8.49 us -> 0 us
  matrix products: 5.45 us -> 0 us
  other arithmetic: 1.94 us -> 0 us
    all_gather x4 -> x0, blocking collectives: 72.7 us -> none  [the longest x1 21.3 us: on_device(): lax.all_gather(keys, 'res', axis=1, tiled=True)]
    pallas_call x0 -> x1, Pallas kernels: none -> 51.8 us  [fused(): pl.pallas_call(functools.partial(kernel, rows, scale), out_shape=(jax.Sha...]
    psum x1 -> x0, waiting for transfers between devices: 19.7 us -> none  [on_device(): tied_sum = lax.psum(partial_logits, 'row') * logit_scale]
    all_to_all x2 -> x0, starting transfers between devices: 8.45 us -> none  [the longest x1 4.46 us: on_device(): lax.all_to_all(score_heads, 'res', split_axis=2, concat_axis=1, tiled=True)]
    dot_general x8 -> x0, matrix products: 5.45 us -> none  [the longest x1 1.15 us: on_device(): jnp.dot(attended, out_weight, preferred_element_type=jnp.float32)]
    reshape x8 -> x0, local copies, waits for them, and re-layouts: 5.17 us -> none  [the longest x1 1.1 us: split_heads(): array.reshape(array.shape[0], array.shape[1], HEADS, array.shape[2] // HE...]
    all_to_all x2 -> x0, waiting for transfers between devices: 4.19 us -> none  [the longest x1 3.55 us: on_device(): lax.all_to_all(score_heads, 'res', split_axis=2, concat_axis=1, tiled=True)]
    all_gather x4 -> x0, local copies, waits for them, and re-layouts: 3.29 us -> none  [the longest x1 1.35 us: on_device(): lax.all_gather(queries, 'res', axis=1, tiled=True)]
  transfers between devices with their start and end apart: 3 -> 0, of which waited for: 3 -> 0; matrix products, arithmetic and copies ran while one was open for 7% -> 0% of each run, Pallas kernels for 0% -> 0%
where the time goes in v2:
time: 57.2 us; the launch traced here: 57 us
  Pallas kernels  51.8 us (91%)
  local copies, waits for them, and re-layouts  4.48 us (8%)
  between operations  0.65 us (1%)
    pallas_call x1, Pallas kernels, fused(): pl.pallas_call(functools.partial(kernel, rows, scale), out_shape=(jax.Sha...  51.8 us
    unnamed x10, local copies, waits for them, and re-layouts  4.48 us

profile of v2, /device:TPU:0, one launch (start us, length us, event | category | flops | bytes accessed | tf_op | source)
XLA Modules:
  0.0 57.0 jit_solution(5522483192459214220)
XLA Ops:
  0.6 51.8 %shard_map.84 = (bf16[4,64,768]{2,1,0:T(8,128)(2,1)}, bf16[4,64,384]{2,1,0:T(8,128)(2,1)}, bf16[4,64,384]{2,1,0:T(8,128)(2,1)}, bf16[4,64,384]{2,1,0:T(8,128)(2,1)}) custom-call(bf16[4,64,384]{2,1,0:T(8,128)(2,1)} %q_ref.1, bf16[4,64,384]{2,1,0:T(8,128)(2,1)} %k_ref.1, bf16[4,64,384]{2,1,0:T(8,128)(2,1)} %v_ref.1, bf16[384,768]{1,0:T(8,128)(2,1)} %w_hbm.1, ...), custom_call_target="tpu_custom_call" | custom-call | tf_op jit(solution)/shard_map/pallas_call | solution.py:400
  52.5 0.0 copy-start.2
  52.5 1.8 %copy.13 = bf16[4,64,768]{2,1,0:T(8,128)(2,1)} copy(bf16[4,64,768]{2,1,0:T(8,128)(2,1)} %get-tuple-element.8) | data formatting | bytes 786432
  54.3 0.0 copy-done.2
  54.3 0.0 copy-start.1
  54.3 0.7 %copy.14 = bf16[4,64,384]{2,1,0:T(8,128)(2,1)} copy(bf16[4,64,384]{2,1,0:T(8,128)(2,1)S(1)} %copy-done.2) | data formatting | bytes 393216
  55.0 0.3 copy-done.1
  55.3 0.0 copy-start
  55.3 0.7 %copy.15 = bf16[4,64,384]{2,1,0:T(8,128)(2,1)} copy(bf16[4,64,384]{2,1,0:T(8,128)(2,1)S(1)} %copy-done.1) | data formatting | bytes 393216
  56.0 0.3 copy-done
  56.3 0.7 %copy.16 = bf16[4,64,384]{2,1,0:T(8,128)(2,1)} copy(bf16[4,64,384]{2,1,0:T(8,128)(2,1)S(1)} %copy-done) | data formatting | bytes 393216
Async XLA Ops:
  52.5 1.8 %copy-start.2 = (bf16[4,64,384]{2,1,0:T(8,128)(2,1)S(1)}, bf16[4,64,384]{2,1,0:T(8,128)(2,1)}, u32[]{:S(2)}) copy-start(bf16[4,64,384]{2,1,0:T(8,128)(2,1)} %get-tuple-element.9) | copy-start | bytes 589828
  54.3 1.0 %copy-start.1 = (bf16[4,64,384]{2,1,0:T(8,128)(2,1)S(1)}, bf16[4,64,384]{2,1,0:T(8,128)(2,1)}, u32[]{:S(2)}) copy-start(bf16[4,64,384]{2,1,0:T(8,128)(2,1)} %get-tuple-element.10) | copy-start | bytes 589828
  55.3 1.0 %copy-start = (bf16[4,64,384]{2,1,0:T(8,128)(2,1)S(1)}, bf16[4,64,384]{2,1,0:T(8,128)(2,1)}, u32[]{:S(2)}) copy-start(bf16[4,64,384]{2,1,0:T(8,128)(2,1)} %get-tuple-element.11) | copy-start | bytes 589828

commit v3 on v2

--- a/solution.py
+++ b/solution.py
@@ -139,6 +139,8 @@
     packed,
     held,
     part,
+    pair_held,
+    chip_part,
     part_held,
     prob,
     sent_out,
@@ -147,6 +149,8 @@
     load_sem,
     zin_send,
     zin_recv,
+    pair_send,
+    pair_recv,
     part_send,
     part_recv,
     prob_send,
@@ -159,7 +163,10 @@
     total = 4 * res
     owned = total // rows
     half = TILE // 2
-    r_partners = [lax.rem(me_r + d, rows) for d in range(1, rows)]
+    chips = rows // 2
+    me_c, me_p = lax.rem(me_r, 2), me_r // 2
+    sibling = me_r + 1 - 2 * me_c
+    chip_ids = [lax.rem(me_p + d, chips) for d in range(1, chips)]
     inputs = (q_ref, k_ref, v_ref)
 
     barrier = pltpu.get_barrier_semaphore()
@@ -167,8 +174,9 @@
         pl.semaphore_signal(
             barrier, inc=1, device_id=(me_r, lax.rem(me_z + d, 4)), device_id_type=MESH
         )
-    for r in r_partners:
-        pl.semaphore_signal(barrier, inc=1, device_id=(r, me_z), device_id_type=MESH)
+    pl.semaphore_signal(barrier, inc=1, device_id=(sibling, me_z), device_id_type=MESH)
+    for p in chip_ids:
+        pl.semaphore_signal(barrier, inc=1, device_id=(2 * p + me_c, me_z), device_id_type=MESH)
 
     loads = [
         pltpu.make_async_copy(x.at[:, :, pl.ds(TILE, TILE)], mid.at[n], load_sem.at[n])
@@ -178,7 +186,7 @@
     loads.append(pltpu.make_async_copy(go_hbm, go_ref, load_sem.at[4]))
     for load in loads:
         load.start()
-    pl.semaphore_wait(barrier, 3 + len(r_partners))
+    pl.semaphore_wait(barrier, 4 + len(chip_ids))
 
     def run(z):
         end = is_end(z)
@@ -252,44 +260,66 @@
             first, zero = first_head(a), jnp.zeros_like(a)
             return [dot_nt(jnp.where(first, a, zero), b), dot_nt(jnp.where(first, zero, a), b)]
 
-        def spread_parts(phase, sums):
+        def pair_parts(phase, sums):
             for h, x in enumerate(sums):
-                part[phase, h] = x.reshape(rows, owned, total)
-            for n, r in enumerate(r_partners):
+                part[phase, h] = x.reshape(chips, 2, owned, total)
+            start(
+                part.at[phase, pl.ds(0, heads), :, 1 - me_c],
+                pair_held.at[phase, pl.ds(0, heads)],
+                pair_send.at[phase],
+                pair_recv.at[phase],
+                (sibling, me_z),
+            )
+
+        def chip_parts(phase):
+            arrived(pair_held.at[phase, pl.ds(0, heads)], pair_recv.at[phase])
+            for h in range(heads):
+                chip_part[phase, h] = part[phase, h, :, me_c] + pair_held[phase, h]
+            for n, p in enumerate(chip_ids):
                 start(
-                    part.at[phase, pl.ds(0, heads), r],
-                    part_held.at[phase, me_r, pl.ds(0, heads)],
+                    chip_part.at[phase, pl.ds(0, heads), p],
+                    part_held.at[phase, me_p, pl.ds(0, heads)],
                     part_send.at[phase, n],
                     part_recv.at[phase, n],
-                    (r, me_z),
+                    (2 * p + me_c, me_z),
                 )
             for h in range(heads):
-                part_held[phase, me_r, h] = part[phase, h, me_r]
+                part_held[phase, me_p, h] = chip_part[phase, h, me_p]
 
         def tied(phase):
-            for n in range(rows - 1):
+            for n in range(chips - 1):
                 arrived(part_held.at[phase, n, pl.ds(0, heads)], part_recv.at[phase, n])
             sums = []
             for h in range(heads):
                 x = part_held[phase, 0, h]
-                for r in range(1, rows):
-                    x = x + part_held[phase, r, h]
+                for p in range(1, chips):
+                    x = x + part_held[phase, p, h]
                 sums.append(x)
             return sums
+
+        def send_prob(phase, n, r, device):
+            block = prob.at[phase, pl.ds(0, heads), r]
+            start(block, block, prob_send.at[phase, n], prob_recv.at[phase, n], (device, me_z))
 
         def spread_probs(phase, values):
             for h, x in enumerate(values):
                 prob[phase, h, me_r] = x.astype(jnp.bfloat16)
-            for n, r in enumerate(r_partners):
-                block = prob.at[phase, pl.ds(0, heads), me_r]
-                start(block, block, prob_send.at[phase, n], prob_recv.at[phase, n], (r, me_z))
+            for n, p in enumerate(chip_ids):
+                send_prob(phase, n, me_r, 2 * p + me_c)
+            send_prob(phase, chips - 1, me_r, sibling)
+
+        def forward_probs(phase):
+            for n in range(chips - 1):
+                r = 2 * lax.rem(me_p + chips - 1 - n, chips) + me_c
+                arrived(prob.at[phase, pl.ds(0, heads), r], prob_recv.at[phase, n])
+                send_prob(phase, chips + n, r, sibling)
 
         def probs(phase):
-            for n in range(rows - 1):
-                arrived(prob.at[phase, pl.ds(0, heads), n], prob_recv.at[phase, n])
+            for n in range(chips - 1, 2 * chips - 1):
+                arrived(prob.at[phase, pl.ds(0, heads), 0], prob_recv.at[phase, n])
             return [prob[phase, h].reshape(total, total) for h in range(heads)]
 
-        def emit(array, dot, weights, x, factor, out_ref):
+        def product(array, dot, weights, x, factor):
             y = dot(weights[0], x)
             if end:
                 y = jnp.where(first_head(y), y, dot(weights[1], x))
@@ -298,6 +328,8 @@
             y = y.astype(jnp.bfloat16)
             for s in range(blocks):
                 sent_out[array, :, s] = y[:, s * TILE : (s + 1) * TILE].reshape(4, res, TILE)
+
+        def send_out(array, out_ref):
             for n, p in enumerate(partners):
                 if end:
                     dst = out_ref.at[:, :, tile_of(z)]
@@ -353,25 +385,32 @@
 
         input_of(0)
         input_of(1)
-        spread_parts(0, partial_sums(rows_of(0), rows_of(1)))
+        pair_parts(0, partial_sums(rows_of(0), rows_of(1)))
+        chip_parts(0)
         send_in(3, ga_ref, True)
         send_in(3, None, False)
         weights = [softmax_rows(x * scale) for x in tied(0)]
         spread_probs(0, weights)
+        forward_probs(0)
 
         input_of(2)
         input_of(3)
         vals, grads = rows_of(2), rows_of(3)
-        spread_parts(1, partial_sums(grads, vals))
-
+        pair_parts(1, partial_sums(grads, vals))
         w16 = probs(0)
-        emit(0, dot_nn, w16, vals, None, att_ref)
+        product(0, dot_nn, w16, vals, None)
+        chip_parts(1)
+        send_out(0, att_ref)
+        product(1, dot_tn, w16, grads, None)
         scores = [score_grad(w, g) for w, g in zip(weights, tied(1))]
         spread_probs(1, scores)
-        emit(1, dot_tn, w16, grads, None, gv_ref)
+        send_out(1, gv_ref)
+        forward_probs(1)
         s16 = probs(1)
-        emit(2, dot_nn, s16, rows_of(1), scale, gq_ref)
-        emit(3, dot_tn, s16, rows_of(0), scale, gk_ref)
+        product(2, dot_nn, s16, rows_of(1), scale)
+        send_out(2, gq_ref)
+        product(3, dot_tn, s16, rows_of(0), scale)
+        send_out(3, gk_ref)
 
         finish(0, att_ref)
         mixed = dot_nn(att_ref[...].reshape(seqs * res, 3 * TILE), w_ref[...])
@@ -386,20 +425,31 @@
         pl.when(me_z == z)(functools.partial(run, z))
 
 
+def copy_out(*refs):
+    ins, outs, sem = refs[:4], refs[4:8], refs[8]
+    copies = [pltpu.make_async_copy(x, y, sem.at[n]) for n, (x, y) in enumerate(zip(ins, outs))]
+    for copy in copies:
+        copy.start()
+    for copy in copies:
+        copy.wait()
+
+
 def fused(rows, queries, keys, values, out_weight, grad_out):
     seqs, res, width = queries.shape
     model_dim = out_weight.shape[1]
     total = 4 * res
     owned = total // rows
+    chips = rows // 2
     scale = 1.0 / math.sqrt(width // HEADS * seqs * rows)
     bf16, f32 = jnp.bfloat16, jnp.float32
     dma = pltpu.SemaphoreType.DMA
     hbm = pl.BlockSpec(memory_space=pltpu.HBM)
     vmem = pl.BlockSpec(memory_space=pltpu.VMEM)
     same = jax.ShapeDtypeStruct(queries.shape, bf16)
-    return pl.pallas_call(
+    shapes = (jax.ShapeDtypeStruct((seqs, res, model_dim), bf16), same, same, same)
+    results = pl.pallas_call(
         functools.partial(kernel, rows, scale),
-        out_shape=(jax.ShapeDtypeStruct((seqs, res, model_dim), bf16), same, same, same),
+        out_shape=tuple(pltpu.VMEM(x.shape, x.dtype) for x in shapes),
         in_specs=[hbm] * 5,
         out_specs=(vmem,) * 4,
         scratch_shapes=[
@@ -409,8 +459,10 @@
             pltpu.VMEM((seqs, res, width), bf16),
             pltpu.VMEM((4, 2, seqs // 2, res, TILE), bf16),
             pltpu.VMEM((4, 4, seqs, res, TILE), bf16),
-            pltpu.VMEM((2, 2, rows, owned, total), f32),
-            pltpu.VMEM((2, rows, 2, owned, total), f32),
+            pltpu.VMEM((2, 2, chips, 2, owned, total), f32),
+            pltpu.VMEM((2, 2, chips, owned, total), f32),
+            pltpu.VMEM((2, 2, chips, owned, total), f32),
+            pltpu.VMEM((2, chips, 2, owned, total), f32),
             pltpu.VMEM((2, 2, rows, owned, total), bf16),
             pltpu.VMEM((4, 4, seqs, res, TILE), bf16),
             pltpu.VMEM((4, 2, seqs // 2, res, TILE), bf16),
@@ -418,8 +470,10 @@
             dma((8,)),
             dma((4, 3)),
             dma((4, 3)),
-            dma((2, rows - 1)),
-            dma((2, rows - 1)),
+            dma((2,)),
+            dma((2,)),
+            dma((2, chips - 1)),
+            dma((2, chips - 1)),
             dma((2, rows - 1)),
             dma((2, rows - 1)),
             dma((4, 3)),
@@ -429,6 +483,13 @@
             collective_id=0, has_side_effects=True, vmem_limit_bytes=62 * 1024 * 1024
         ),
     )(queries, keys, values, out_weight, grad_out)
+    return pl.pallas_call(
+        copy_out,
+        out_shape=shapes,
+        in_specs=[pl.BlockSpec(memory_space=pl.ANY)] * 4,
+        out_specs=(pl.BlockSpec(memory_space=pl.ANY),) * 4,
+        scratch_shapes=[dma((4,))],
+    )(*results)
 
 
 def fits(rows, cols, seqs, res, width):
@@ -436,6 +497,7 @@
     return (
         cols == 4
         and rows > 1
+        and rows % 2 == 0
         and seqs == 4
         and width == HEADS * 64
         and res % 16 == 0

time: 57.2 us -> 83.7 us (1.46)
  Pallas kernels: 51.8 us -> 79.7 us
  local copies, waits for them, and re-layouts: 4.48 us -> 2.79 us
    pallas_call x1 -> x2, Pallas kernels: 51.8 us -> 79.7 us  [the longest x1 48.8 us: fused(): pl.pallas_call(functools.partial(kernel, rows, scale), out_shape=tuple((p...]
    unnamed x10 -> x8, local copies, waits for them, and re-layouts: 4.48 us -> 2.79 us
where the time goes in v3:
time: 83.7 us; the launch traced here: 83.1 us
  Pallas kernels  79.7 us (95%)
  local copies, waits for them, and re-layouts  2.79 us (3%)
    pallas_call x1, Pallas kernels, fused(): pl.pallas_call(functools.partial(kernel, rows, scale), out_shape=tuple((p...  48.8 us
    pallas_call x1, Pallas kernels, fused(): pl.pallas_call(copy_out, out_shape=shapes, in_specs=[pl.BlockSpec(memory_...  30.9 us
    unnamed x8, local copies, waits for them, and re-layouts  2.79 us

profile of v3, /device:TPU:0, one launch (start us, length us, event | category | flops | bytes accessed | tf_op | source)
XLA Modules:
  0.0 83.1 jit_solution(10436412402829269186)
XLA Ops:
  0.6 48.8 %shard_map.84 = (bf16[4,64,768]{2,1,0:T(8,128)(2,1)S(1)}, bf16[4,64,384]{2,1,0:T(8,128)(2,1)S(1)}, bf16[4,64,384]{2,1,0:T(8,128)(2,1)S(1)}, bf16[4,64,384]{2,1,0:T(8,128)(2,1)S(1)}) custom-call(bf16[4,64,384]{2,1,0:T(8,128)(2,1)} %q_ref.1, bf16[4,64,384]{2,1,0:T(8,128)(2,1)} %k_ref.1, bf16[4,64,384]{2,1,0:T(8,128)(2,1)} %v_ref.1, bf16[384,768]{1,0:T(8,128)(2,1)} %w_hbm.1, ...), custom_call_target="tpu_custom_call" | custom-call | tf_op jit(solution)/shard_map/pallas_call | solution.py:450
  49.4 0.0 copy-start
  49.4 0.7 copy-done
  50.1 0.0 copy-start.1
  50.1 0.7 copy-done.1
  50.8 0.0 copy-start.2
  50.8 0.7 copy-done.2
  51.5 0.0 copy-start.3
  51.5 0.7 copy-done.3
  52.2 30.9 %shard_map.85 = (bf16[4,64,768]{2,1,0:T(8,128)(2,1)}, bf16[4,64,384]{2,1,0:T(8,128)(2,1)}, bf16[4,64,384]{2,1,0:T(8,128)(2,1)}, bf16[4,64,384]{2,1,0:T(8,128)(2,1)}) custom-call(bf16[4,64,768]{2,1,0:T(8,128)(2,1)} %copy-done, bf16[4,64,384]{2,1,0:T(8,128)(2,1)} %copy-done.1, bf16[4,64,384]{2,1,0:T(8,128)(2,1)} %copy-done.2, bf16[4,64,384]{2,1,0:T(8,128)(2,1)} %copy-done.3), custom_call_target="tpu_custom_call" | custom-call | tf_op jit(solution)/shard_map/pallas_call | solution.py:486
Async XLA Ops:
  49.4 0.7 copy-start
  50.1 0.7 copy-start.1
  50.8 0.7 copy-start.2
  51.5 0.7 copy-start.3

commit v4 on v3

--- a/solution.py
+++ b/solution.py
@@ -176,7 +176,8 @@
         )
     pl.semaphore_signal(barrier, inc=1, device_id=(sibling, me_z), device_id_type=MESH)
     for p in chip_ids:
-        pl.semaphore_signal(barrier, inc=1, device_id=(2 * p + me_c, me_z), device_id_type=MESH)
+        for c in range(2):
+            pl.semaphore_signal(barrier, inc=1, device_id=(2 * p + c, me_z), device_id_type=MESH)
 
     loads = [
         pltpu.make_async_copy(x.at[:, :, pl.ds(TILE, TILE)], mid.at[n], load_sem.at[n])
@@ -186,7 +187,7 @@
     loads.append(pltpu.make_async_copy(go_hbm, go_ref, load_sem.at[4]))
     for load in loads:
         load.start()
-    pl.semaphore_wait(barrier, 4 + len(chip_ids))
+    pl.semaphore_wait(barrier, 4 + 2 * len(chip_ids))
 
     def run(z):
         end = is_end(z)
@@ -307,6 +308,9 @@
             for n, p in enumerate(chip_ids):
                 send_prob(phase, n, me_r, 2 * p + me_c)
             send_prob(phase, chips - 1, me_r, sibling)
+            if phase == 1:
+                for n, p in enumerate(chip_ids):
+                    send_prob(phase, chips + n, me_r, 2 * p + 1 - me_c)
 
         def forward_probs(phase):
             for n in range(chips - 1):
@@ -315,7 +319,7 @@
                 send_prob(phase, chips + n, r, sibling)
 
         def probs(phase):
-            for n in range(chips - 1, 2 * chips - 1):
+            for n in range(chips - 1 if phase == 0 else 0, 2 * chips - 1):
                 arrived(prob.at[phase, pl.ds(0, heads), 0], prob_recv.at[phase, n])
             return [prob[phase, h].reshape(total, total) for h in range(heads)]
 
@@ -405,7 +409,6 @@
         scores = [score_grad(w, g) for w, g in zip(weights, tied(1))]
         spread_probs(1, scores)
         send_out(1, gv_ref)
-        forward_probs(1)
         s16 = probs(1)
         product(2, dot_nn, s16, rows_of(1), scale)
         send_out(2, gq_ref)
@@ -486,9 +489,10 @@
     return pl.pallas_call(
         copy_out,
         out_shape=shapes,
-        in_specs=[pl.BlockSpec(memory_space=pl.ANY)] * 4,
+        in_specs=[vmem] * 4,
         out_specs=(pl.BlockSpec(memory_space=pl.ANY),) * 4,
         scratch_shapes=[dma((4,))],
+        compiler_params=pltpu.CompilerParams(vmem_limit_bytes=2 * 1024 * 1024),
     )(*results)
 
 

time: 83.7 us -> 52.6 us (0.63)
  Pallas kernels: 79.7 us -> 51.8 us
  local copies, waits for them, and re-layouts: 2.79 us -> 0 us
    pallas_call x1, Pallas kernels: 30.9 us -> 0.97 us  [fused(): pl.pallas_call(copy_out, out_shape=shapes, in_specs=[vmem] * 4, out_specs...]
    unnamed x8 -> x0, local copies, waits for them, and re-layouts: 2.79 us -> none
    pallas_call x1, Pallas kernels: 48.8 us -> 50.8 us  [fused(): pl.pallas_call(functools.partial(kernel, rows, scale), out_shape=tuple((p...]
where the time goes in v4:
time: 52.6 us; the launch traced here: 52.5 us
  Pallas kernels  51.8 us (98%)
  between operations  0.64 us (1%)
    pallas_call x1, Pallas kernels, fused(): pl.pallas_call(functools.partial(kernel, rows, scale), out_shape=tuple((p...  50.8 us

profile of v4, /device:TPU:0, one launch (start us, length us, event | category | flops | bytes accessed | tf_op | source)
XLA Modules:
  0.0 52.5 jit_solution(33865296818423018)
XLA Ops:
  0.6 50.8 %shard_map.84 = (bf16[4,64,768]{2,1,0:T(8,128)(2,1)S(1)}, bf16[4,64,384]{2,1,0:T(8,128)(2,1)S(1)}, bf16[4,64,384]{2,1,0:T(8,128)(2,1)S(1)}, bf16[4,64,384]{2,1,0:T(8,128)(2,1)S(1)}) custom-call(bf16[4,64,384]{2,1,0:T(8,128)(2,1)} %q_ref.1, bf16[4,64,384]{2,1,0:T(8,128)(2,1)} %k_ref.1, bf16[4,64,384]{2,1,0:T(8,128)(2,1)} %v_ref.1, bf16[384,768]{1,0:T(8,128)(2,1)} %w_hbm.1, ...), custom_call_target="tpu_custom_call" | custom-call | tf_op jit(solution)/shard_map/pallas_call | solution.py:453
  51.5 1.0 %shard_map.85 = (bf16[4,64,768]{2,1,0:T(8,128)(2,1)}, bf16[4,64,384]{2,1,0:T(8,128)(2,1)}, bf16[4,64,384]{2,1,0:T(8,128)(2,1)}, bf16[4,64,384]{2,1,0:T(8,128)(2,1)}) custom-call(bf16[4,64,768]{2,1,0:T(8,128)(2,1)S(1)} %get-tuple-element.8.refs_0_, bf16[4,64,384]{2,1,0:T(8,128)(2,1)S(1)} %get-tuple-element.9.refs_1_, ...), custom_call_target="tpu_custom_call" | custom-call | tf_op jit(solution)/shard_map/pallas_call | solution.py:489

commit v5 on v3

--- a/solution.py
+++ b/solution.py
@@ -369,10 +369,8 @@
             loads[n].wait()
             pack(n, [mid[n, s] for s in range(seqs)])
             send_in(n, None, False)
-        send_in(2, v_ref, True)
         loads[2].wait()
         pack(2, [mid[2, s] for s in range(seqs)])
-        send_in(2, None, False)
         loads[3].wait()
         loads[4].wait()
         ga = dot_nt(go_ref[...].reshape(seqs * res, go_ref.shape[2]), w_ref[...])
@@ -383,6 +381,10 @@
             held[3, z] = ga[:, :, lo : lo + TILE]
         pack(3, [ga[s, :, TILE : 2 * TILE] for s in range(seqs)])
 
+        while pending:
+            pending.pop(0).wait_send()
+        send_in(2, v_ref, True)
+        send_in(2, None, False)
         input_of(0)
         input_of(1)
         pair_parts(0, partial_sums(rows_of(0), rows_of(1)))
@@ -399,12 +401,12 @@
         pair_parts(1, partial_sums(grads, vals))
         w16 = probs(0)
         product(0, dot_nn, w16, vals, None)
+        send_out(0, att_ref)
         chip_parts(1)
-        send_out(0, att_ref)
         product(1, dot_tn, w16, grads, None)
+        send_out(1, gv_ref)
         scores = [score_grad(w, g) for w, g in zip(weights, tied(1))]
         spread_probs(1, scores)
-        send_out(1, gv_ref)
         forward_probs(1)
         s16 = probs(1)
         product(2, dot_nn, s16, rows_of(1), scale)
@@ -486,9 +488,10 @@
     return pl.pallas_call(
         copy_out,
         out_shape=shapes,
-        in_specs=[pl.BlockSpec(memory_space=pl.ANY)] * 4,
+        in_specs=[vmem] * 4,
         out_specs=(pl.BlockSpec(memory_space=pl.ANY),) * 4,
         scratch_shapes=[dma((4,))],
+        compiler_params=pltpu.CompilerParams(vmem_limit_bytes=2 * 1024 * 1024),
     )(*results)
 
 

time: 83.7 us -> 50.9 us (0.61)
  Pallas kernels: 79.7 us -> 49.7 us
  local copies, waits for them, and re-layouts: 2.79 us -> 0 us
    pallas_call x1, Pallas kernels: 30.9 us -> 0.97 us  [fused(): pl.pallas_call(copy_out, out_shape=shapes, in_specs=[vmem] * 4, out_specs...]
    unnamed x8 -> x0, local copies, waits for them, and re-layouts: 2.79 us -> none
where the time goes in v5:
time: 50.9 us; the launch traced here: 50.3 us
  Pallas kernels  49.7 us (98%)
  between operations  0.64 us (1%)
    pallas_call x1, Pallas kernels, fused(): pl.pallas_call(functools.partial(kernel, rows, scale), out_shape=tuple((p...  48.7 us

profile of v5, /device:TPU:0, one launch (start us, length us, event | category | flops | bytes accessed | tf_op | source)
XLA Modules:
  0.0 50.3 jit_solution(4473811717817692244)
XLA Ops:
  0.6 48.7 %shard_map.84 = (bf16[4,64,768]{2,1,0:T(8,128)(2,1)S(1)}, bf16[4,64,384]{2,1,0:T(8,128)(2,1)S(1)}, bf16[4,64,384]{2,1,0:T(8,128)(2,1)S(1)}, bf16[4,64,384]{2,1,0:T(8,128)(2,1)S(1)}) custom-call(bf16[4,64,384]{2,1,0:T(8,128)(2,1)} %q_ref.1, bf16[4,64,384]{2,1,0:T(8,128)(2,1)} %k_ref.1, bf16[4,64,384]{2,1,0:T(8,128)(2,1)} %v_ref.1, bf16[384,768]{1,0:T(8,128)(2,1)} %w_hbm.1, ...), custom_call_target="tpu_custom_call" | custom-call | tf_op jit(solution)/shard_map/pallas_call | solution.py:452
  49.4 1.0 %shard_map.85 = (bf16[4,64,768]{2,1,0:T(8,128)(2,1)}, bf16[4,64,384]{2,1,0:T(8,128)(2,1)}, bf16[4,64,384]{2,1,0:T(8,128)(2,1)}, bf16[4,64,384]{2,1,0:T(8,128)(2,1)}) custom-call(bf16[4,64,768]{2,1,0:T(8,128)(2,1)S(1)} %get-tuple-element.8.refs_0_, bf16[4,64,384]{2,1,0:T(8,128)(2,1)S(1)} %get-tuple-element.9.refs_1_, ...), custom_call_target="tpu_custom_call" | custom-call | tf_op jit(solution)/shard_map/pallas_call | solution.py:488

commit v6 on v5

--- a/solution.py
+++ b/solution.py
@@ -263,34 +263,33 @@
         def pair_parts(phase, sums):
             for h, x in enumerate(sums):
                 part[phase, h] = x.reshape(chips, 2, owned, total)
-            start(
-                part.at[phase, pl.ds(0, heads), :, 1 - me_c],
-                pair_held.at[phase, pl.ds(0, heads)],
-                pair_send.at[phase],
-                pair_recv.at[phase],
-                (sibling, me_z),
-            )
+                start(
+                    part.at[phase, h, :, 1 - me_c],
+                    pair_held.at[phase, h],
+                    pair_send.at[phase, h],
+                    pair_recv.at[phase, h],
+                    (sibling, me_z),
+                )
 
         def chip_parts(phase):
-            arrived(pair_held.at[phase, pl.ds(0, heads)], pair_recv.at[phase])
             for h in range(heads):
+                arrived(pair_held.at[phase, h], pair_recv.at[phase, h])
                 chip_part[phase, h] = part[phase, h, :, me_c] + pair_held[phase, h]
-            for n, p in enumerate(chip_ids):
-                start(
-                    chip_part.at[phase, pl.ds(0, heads), p],
-                    part_held.at[phase, me_p, pl.ds(0, heads)],
-                    part_send.at[phase, n],
-                    part_recv.at[phase, n],
-                    (2 * p + me_c, me_z),
-                )
-            for h in range(heads):
+                for n, p in enumerate(chip_ids):
+                    start(
+                        chip_part.at[phase, h, p],
+                        part_held.at[phase, me_p, h],
+                        part_send.at[phase, h, n],
+                        part_recv.at[phase, h, n],
+                        (2 * p + me_c, me_z),
+                    )
                 part_held[phase, me_p, h] = chip_part[phase, h, me_p]
 
         def tied(phase):
-            for n in range(chips - 1):
-                arrived(part_held.at[phase, n, pl.ds(0, heads)], part_recv.at[phase, n])
             sums = []
             for h in range(heads):
+                for n in range(chips - 1):
+                    arrived(part_held.at[phase, n, h], part_recv.at[phase, h, n])
                 x = part_held[phase, 0, h]
                 for p in range(1, chips):
                     x = x + part_held[phase, p, h]
@@ -385,12 +384,12 @@
             pending.pop(0).wait_send()
         send_in(2, v_ref, True)
         send_in(2, None, False)
+        send_in(3, ga_ref, True)
+        send_in(3, None, False)
         input_of(0)
         input_of(1)
         pair_parts(0, partial_sums(rows_of(0), rows_of(1)))
         chip_parts(0)
-        send_in(3, ga_ref, True)
-        send_in(3, None, False)
         weights = [softmax_rows(x * scale) for x in tied(0)]
         spread_probs(0, weights)
         forward_probs(0)
@@ -472,10 +471,10 @@
             dma((8,)),
             dma((4, 3)),
             dma((4, 3)),
-            dma((2,)),
-            dma((2,)),
-            dma((2, chips - 1)),
-            dma((2, chips - 1)),
+            dma((2, 2)),
+            dma((2, 2)),
+            dma((2, 2, chips - 1)),
+            dma((2, 2, chips - 1)),
             dma((2, rows - 1)),
             dma((2, rows - 1)),
             dma((4, 3)),

time: 50.9 us -> 52.7 us (1.035)
  Pallas kernels: 49.7 us -> 51.9 us
    pallas_call x1, Pallas kernels: 48.7 us -> 50.9 us  [fused(): pl.pallas_call(functools.partial(kernel, rows, scale), out_shape=tuple((p...]
where the time goes in v6:
time: 52.7 us; the launch traced here: 52.5 us
  Pallas kernels  51.9 us (98%)
  between operations  0.64 us (1%)
    pallas_call x1, Pallas kernels, fused(): pl.pallas_call(functools.partial(kernel, rows, scale), out_shape=tuple((p...  50.9 us

profile of v6, /device:TPU:0, one launch (start us, length us, event | category | flops | bytes accessed | tf_op | source)
XLA Modules:
  0.0 52.5 jit_solution(11016295746885458441)
XLA Ops:
  0.6 50.9 %shard_map.84 = (bf16[4,64,768]{2,1,0:T(8,128)(2,1)S(1)}, bf16[4,64,384]{2,1,0:T(8,128)(2,1)S(1)}, bf16[4,64,384]{2,1,0:T(8,128)(2,1)S(1)}, bf16[4,64,384]{2,1,0:T(8,128)(2,1)S(1)}) custom-call(bf16[4,64,384]{2,1,0:T(8,128)(2,1)} %q_ref.1, bf16[4,64,384]{2,1,0:T(8,128)(2,1)} %k_ref.1, bf16[4,64,384]{2,1,0:T(8,128)(2,1)} %v_ref.1, bf16[384,768]{1,0:T(8,128)(2,1)} %w_hbm.1, ...), custom_call_target="tpu_custom_call" | custom-call | tf_op jit(solution)/shard_map/pallas_call | solution.py:451
  51.6 1.0 %shard_map.85 = (bf16[4,64,768]{2,1,0:T(8,128)(2,1)}, bf16[4,64,384]{2,1,0:T(8,128)(2,1)}, bf16[4,64,384]{2,1,0:T(8,128)(2,1)}, bf16[4,64,384]{2,1,0:T(8,128)(2,1)}) custom-call(bf16[4,64,768]{2,1,0:T(8,128)(2,1)S(1)} %get-tuple-element.8.refs_0_, bf16[4,64,384]{2,1,0:T(8,128)(2,1)S(1)} %get-tuple-element.9.refs_1_, ...), custom_call_target="tpu_custom_call" | custom-call | tf_op jit(solution)/shard_map/pallas_call | solution.py:487

commit v7 on v5

--- a/solution.py
+++ b/solution.py
@@ -329,8 +329,9 @@
             for s in range(blocks):
                 sent_out[array, :, s] = y[:, s * TILE : (s + 1) * TILE].reshape(4, res, TILE)
 
-        def send_out(array, out_ref):
-            for n, p in enumerate(partners):
+        def send_out(array, out_ref, some=range(3)):
+            for n in some:
+                p = partners[n]
                 if end:
                     dst = out_ref.at[:, :, tile_of(z)]
                 else:
@@ -342,6 +343,8 @@
                     zout_recv.at[array, n],
                     (me_r, p),
                 )
+            if some[0] > 0:
+                return
             if end:
                 lo = 0 if z == 0 else 2 * TILE
                 out_ref[:, :, lo : lo + TILE] = sent_out[array, z]
@@ -384,15 +387,15 @@
         while pending:
             pending.pop(0).wait_send()
         send_in(2, v_ref, True)
-        send_in(2, None, False)
         input_of(0)
         input_of(1)
         pair_parts(0, partial_sums(rows_of(0), rows_of(1)))
+        send_in(2, None, False)
         chip_parts(0)
         send_in(3, ga_ref, True)
-        send_in(3, None, False)
         weights = [softmax_rows(x * scale) for x in tied(0)]
         spread_probs(0, weights)
+        send_in(3, None, False)
         forward_probs(0)
 
         input_of(2)
@@ -401,13 +404,14 @@
         pair_parts(1, partial_sums(grads, vals))
         w16 = probs(0)
         product(0, dot_nn, w16, vals, None)
+        chip_parts(1)
         send_out(0, att_ref)
-        chip_parts(1)
         product(1, dot_tn, w16, grads, None)
-        send_out(1, gv_ref)
         scores = [score_grad(w, g) for w, g in zip(weights, tied(1))]
         spread_probs(1, scores)
+        send_out(1, gv_ref, range(1))
         forward_probs(1)
+        send_out(1, gv_ref, range(1, 3))
         s16 = probs(1)
         product(2, dot_nn, s16, rows_of(1), scale)
         send_out(2, gq_ref)

time: 50.9 us -> 53.7 us (1.055)
  Pallas kernels: 49.7 us -> 52.9 us
    pallas_call x1, Pallas kernels: 48.7 us -> 51.9 us  [fused(): pl.pallas_call(functools.partial(kernel, rows, scale), out_shape=tuple((p...]
where the time goes in v7:
time: 53.7 us; the launch traced here: 53.5 us
  Pallas kernels  52.9 us (99%)
  between operations  0.64 us (1%)
    pallas_call x1, Pallas kernels, fused(): pl.pallas_call(functools.partial(kernel, rows, scale), out_shape=tuple((p...  51.9 us

profile of v7, /device:TPU:0, one launch (start us, length us, event | category | flops | bytes accessed | tf_op | source)
XLA Modules:
  0.0 53.5 jit_solution(18283683807114537306)
XLA Ops:
  0.6 51.9 %shard_map.84 = (bf16[4,64,768]{2,1,0:T(8,128)(2,1)S(1)}, bf16[4,64,384]{2,1,0:T(8,128)(2,1)S(1)}, bf16[4,64,384]{2,1,0:T(8,128)(2,1)S(1)}, bf16[4,64,384]{2,1,0:T(8,128)(2,1)S(1)}) custom-call(bf16[4,64,384]{2,1,0:T(8,128)(2,1)} %q_ref.1, bf16[4,64,384]{2,1,0:T(8,128)(2,1)} %k_ref.1, bf16[4,64,384]{2,1,0:T(8,128)(2,1)} %v_ref.1, bf16[384,768]{1,0:T(8,128)(2,1)} %w_hbm.1, ...), custom_call_target="tpu_custom_call" | custom-call | tf_op jit(solution)/shard_map/pallas_call | solution.py:456
  52.5 1.0 %shard_map.85 = (bf16[4,64,768]{2,1,0:T(8,128)(2,1)}, bf16[4,64,384]{2,1,0:T(8,128)(2,1)}, bf16[4,64,384]{2,1,0:T(8,128)(2,1)}, bf16[4,64,384]{2,1,0:T(8,128)(2,1)}) custom-call(bf16[4,64,768]{2,1,0:T(8,128)(2,1)S(1)} %get-tuple-element.8.refs_0_, bf16[4,64,384]{2,1,0:T(8,128)(2,1)S(1)} %get-tuple-element.9.refs_1_, ...), custom_call_target="tpu_custom_call" | custom-call | tf_op jit(solution)/shard_map/pallas_call | solution.py:492

commit v8 on v5

--- a/solution.py
+++ b/solution.py
@@ -369,8 +369,10 @@
             loads[n].wait()
             pack(n, [mid[n, s] for s in range(seqs)])
             send_in(n, None, False)
+        send_in(2, v_ref, True)
         loads[2].wait()
         pack(2, [mid[2, s] for s in range(seqs)])
+        send_in(2, None, False)
         loads[3].wait()
         loads[4].wait()
         ga = dot_nt(go_ref[...].reshape(seqs * res, go_ref.shape[2]), w_ref[...])
@@ -381,10 +383,6 @@
             held[3, z] = ga[:, :, lo : lo + TILE]
         pack(3, [ga[s, :, TILE : 2 * TILE] for s in range(seqs)])
 
-        while pending:
-            pending.pop(0).wait_send()
-        send_in(2, v_ref, True)
-        send_in(2, None, False)
         input_of(0)
         input_of(1)
         pair_parts(0, partial_sums(rows_of(0), rows_of(1)))

time: 50.9 us -> 50.9 us (level)
  no operation moved by 1% of the time
where the time goes in v8:
time: 50.9 us; the launch traced here: 50.3 us
  Pallas kernels  49.7 us (98%)
  between operations  0.64 us (1%)
    pallas_call x1, Pallas kernels, fused(): pl.pallas_call(functools.partial(kernel, rows, scale), out_shape=tuple((p...  48.7 us

profile of v8, /device:TPU:0, one launch (start us, length us, event | category | flops | bytes accessed | tf_op | source)
XLA Modules:
  0.0 50.3 jit_solution(16257305119778933661)
XLA Ops:
  0.6 48.7 %shard_map.84 = (bf16[4,64,768]{2,1,0:T(8,128)(2,1)S(1)}, bf16[4,64,384]{2,1,0:T(8,128)(2,1)S(1)}, bf16[4,64,384]{2,1,0:T(8,128)(2,1)S(1)}, bf16[4,64,384]{2,1,0:T(8,128)(2,1)S(1)}) custom-call(bf16[4,64,384]{2,1,0:T(8,128)(2,1)} %q_ref.1, bf16[4,64,384]{2,1,0:T(8,128)(2,1)} %k_ref.1, bf16[4,64,384]{2,1,0:T(8,128)(2,1)} %v_ref.1, bf16[384,768]{1,0:T(8,128)(2,1)} %w_hbm.1, ...), custom_call_target="tpu_custom_call" | custom-call | tf_op jit(solution)/shard_map/pallas_call | solution.py:450
  49.4 1.0 %shard_map.85 = (bf16[4,64,768]{2,1,0:T(8,128)(2,1)}, bf16[4,64,384]{2,1,0:T(8,128)(2,1)}, bf16[4,64,384]{2,1,0:T(8,128)(2,1)}, bf16[4,64,384]{2,1,0:T(8,128)(2,1)}) custom-call(bf16[4,64,768]{2,1,0:T(8,128)(2,1)S(1)} %get-tuple-element.8.refs_0_, bf16[4,64,384]{2,1,0:T(8,128)(2,1)S(1)} %get-tuple-element.9.refs_1_, ...), custom_call_target="tpu_custom_call" | custom-call | tf_op jit(solution)/shard_map/pallas_call | solution.py:486
